TPU v7x, 32 devices: a whole 2x2x4 slice. The times are simulated.
32 devices in a mesh: section: 2 (over core), head: 4 (over z), blk: 4 (over y, x).
Axes of the slice: x: 2, y: 2, z: 4, core: 2. Of those that a mesh axis runs over, the one named last changes fastest.
Arguments:
- section_input: bfloat16 [2, 8, 256, 1536], P('section', 'blk')
- modulation: bfloat16 [2, 8, 2, 1536], P('section', 'blk'), may hold values from -3 to 3
- attn_gate: bfloat16 [2, 8, 1536], P('section', 'blk'), may hold values from -12 to 12
- qkv_weight: bfloat16 [2, 1536, 3, 1536], P('section', None, None, 'head'), may hold values from -0.15625 to 0.15625
- out_weight: bfloat16 [2, 1536, 1536], P('section', 'head'), may hold values from -0.15625 to 0.15625
- kv_cache: bfloat16 [2, 8, 256, 4, 2, 1536], P('section', None, 'blk', None, None, 'head'), may hold values from -9 to 9
- text_kv: bfloat16 [2, 8, 154, 2, 1536], P('section', 'blk', None, None, 'head')
- text_len: int32 [8], P('blk'), may hold values from 4 to 154, as said below
- patch_order: int32 [4, 4], replicated, may hold values from 0 to 3, each once within a row
- final_mod: bfloat16 [8, 2, 1536], P('blk'), may hold values from -3 to 3
- final_weight: bfloat16 [1536, 64], replicated, may hold values from -0.15625 to 0.15625
- latent: float32 [4, 128, 128], P('blk', 'section'), may hold values from -6 to 6
Outputs:
- section_output: bfloat16 [2, 8, 256, 1536], P('section', 'blk', None, 'head')
- cache_patch: bfloat16 [2, 8, 256, 2, 1536], P('section', None, 'blk', None, 'head')
- latent_next: float32 [4, 128, 128], P('blk', 'section')
Inputs may be any that keep to these rules, and one draw needn't show every extreme that they name: `text_len`: sequence 0 uses all 154 text positions. `patch_order`: each row is a permutation of the 4 patches.
All inputs are finite; a program needn't handle non-finite values.
Results may differ from a plain program's by a relative error of at most 0.0092.
Values may be sent and summed in bfloat16 or wider, within the bound.
A program may use at most 128 MiB of HBM per device.

v0:
```python
import jax
import jax.numpy as jnp
from jax import lax
from jax.sharding import PartitionSpec as P

HEAD_DIM = 64


norm_eps = 1e-06
guidance = 4.0
euler_step = -0.25


def passed_along(shard, axis, by):
    devices = lax.axis_size(axis)
    return lax.ppermute(shard, axis, [(i, (i + by) % devices) for i in range(devices)])


def layer_norm(values):
    row_mean = jnp.mean(values, axis=-1, keepdims=True)
    centered = values - row_mean
    row_var = jnp.mean(centered * centered, axis=-1, keepdims=True)
    return centered / jnp.sqrt(row_var + norm_eps)


def piece_scores(query_heads, key_piece, counted_piece):
    seq_dev = key_piece.shape[0]
    head_count = query_heads.shape[2]
    key_heads = key_piece.reshape(seq_dev, -1, head_count, HEAD_DIM)
    scores = jnp.einsum(
        "sqhd,skhd->shqk", query_heads, key_heads, preferred_element_type=jnp.float32
    ) * HEAD_DIM ** (-0.5)
    if counted_piece is not None:
        scores = jnp.where(counted_piece[:, None, None, :], scores, -1e30)
    return scores


def piece_values(probs_piece, value_piece, head_count):
    seq_dev = value_piece.shape[0]
    value_heads = value_piece.reshape(seq_dev, -1, head_count, HEAD_DIM)
    return jnp.einsum(
        "shqk,skhd->sqhd", probs_piece, value_heads, preferred_element_type=jnp.float32
    )


def shards(
    section_input,
    modulation,
    attn_gate,
    qkv_weight,
    out_weight,
    kv_cache,
    text_kv,
    text_len,
    patch_order,
    final_mod,
    final_weight,
    latent,
):
    section_index = lax.axis_index("section")
    seq_patch = jnp.repeat(
        lax.dynamic_index_in_dim(patch_order, section_index, 1, keepdims=False), 2
    )
    hidden_in = section_input[0]
    seq_dev, patch_rows, model_width = hidden_in.shape
    own_patch = lax.dynamic_slice_in_dim(seq_patch, lax.axis_index("blk") * seq_dev, seq_dev, 0)
    hidden_wide = hidden_in.astype(jnp.float32)
    shift_scale = modulation[0].astype(jnp.float32)
    normed = (layer_norm(hidden_wide) * (1.0 + shift_scale[:, 1:2]) + shift_scale[:, 0:1]).astype(
        jnp.bfloat16
    )
    group_width = qkv_weight.shape[3]
    projected = jnp.dot(
        normed.reshape(seq_dev * patch_rows, model_width),
        qkv_weight[0].reshape(model_width, 3 * group_width),
        preferred_element_type=jnp.float32,
    ).astype(jnp.bfloat16)
    projected = projected.reshape(seq_dev, patch_rows, 3, group_width)
    queries = projected[:, :, 0]
    key_new = projected[:, :, 1]
    value_new = projected[:, :, 2]
    fresh_kv = jnp.stack([key_new, value_new], axis=2)
    refreshed = lax.all_to_all(fresh_kv, "blk", split_axis=1, concat_axis=0, tiled=True)
    local_cache = kv_cache[0]
    patch_count = local_cache.shape[2]
    fetched = lax.all_to_all(local_cache, "blk", split_axis=0, concat_axis=1, tiled=True)
    keep_patch = jnp.arange(patch_count, dtype=jnp.int32)[None, :] != own_patch[:, None]
    stale_counted = jnp.tile(keep_patch, (1, patch_rows))
    stale_keys = fetched[:, :, :, 0].reshape(seq_dev, -1, group_width)
    stale_values = fetched[:, :, :, 1].reshape(seq_dev, -1, group_width)
    text_local = text_kv[0]
    text_count = text_local.shape[1]
    text_counted = jnp.arange(text_count, dtype=jnp.int32)[None, :] < text_len[:, None]
    head_count = group_width // HEAD_DIM
    query_heads = queries.reshape(seq_dev, patch_rows, head_count, HEAD_DIM)
    text_scores = piece_scores(query_heads, text_local[:, :, 0], text_counted)
    fresh_scores = piece_scores(query_heads, key_new, None)
    stale_scores = piece_scores(query_heads, stale_keys, stale_counted)
    row_max = jnp.maximum(
        jnp.maximum(
            jnp.max(text_scores, axis=-1, keepdims=True),
            jnp.max(fresh_scores, axis=-1, keepdims=True),
        ),
        jnp.max(stale_scores, axis=-1, keepdims=True),
    )
    text_weights = jnp.exp(text_scores - row_max)
    fresh_weights = jnp.exp(fresh_scores - row_max)
    stale_weights = jnp.exp(stale_scores - row_max)
    total = (
        jnp.sum(text_weights, axis=-1, keepdims=True)
        + jnp.sum(fresh_weights, axis=-1, keepdims=True)
        + jnp.sum(stale_weights, axis=-1, keepdims=True)
    )
    text_probs = (text_weights / total).astype(jnp.bfloat16)
    fresh_probs = (fresh_weights / total).astype(jnp.bfloat16)
    stale_probs = (stale_weights / total).astype(jnp.bfloat16)
    attended_wide = (
        piece_values(text_probs, text_local[:, :, 1], head_count)
        + piece_values(fresh_probs, value_new, head_count)
        + piece_values(stale_probs, stale_values, head_count)
    )
    attended = attended_wide.astype(jnp.bfloat16)
    partial_value = jnp.dot(
        attended.reshape(seq_dev * patch_rows, group_width),
        out_weight[0],
        preferred_element_type=jnp.float32,
    )
    gate_wide = attn_gate[0].astype(jnp.float32)[:, None, :]
    share_width = model_width // lax.axis_size("head")
    share_start = lax.axis_index("head") * share_width
    half_rows = patch_rows // 2
    share_sum = lax.psum_scatter(
        partial_value.reshape(seq_dev, patch_rows, model_width).astype(jnp.bfloat16),
        "head",
        scatter_dimension=2,
        tiled=True,
    ).astype(jnp.float32)
    own_hidden = lax.dynamic_slice_in_dim(hidden_wide, share_start, share_width, 2)
    own_gate = lax.dynamic_slice_in_dim(gate_wide, share_start, share_width, 2)
    layer_out = (own_hidden + own_gate * share_sum).astype(jnp.bfloat16)
    received = passed_along(layer_out, "section", 1)
    last_layer = jnp.where(section_index == 0, received, layer_out)
    last_half = lax.dynamic_slice_in_dim(last_layer, section_index * half_rows, half_rows, 1)
    final_rows = lax.all_gather(last_half, "head", axis=2, tiled=True)
    final_shift = final_mod.astype(jnp.float32)
    final_normed = (
        layer_norm(final_rows.astype(jnp.float32)) * (1.0 + final_shift[:, 1:2])
        + final_shift[:, 0:1]
    ).astype(jnp.bfloat16)
    velocity = jnp.dot(
        final_normed.reshape(seq_dev * half_rows, model_width),
        final_weight,
        preferred_element_type=jnp.float32,
    )
    velocity = velocity.reshape(seq_dev // 2, 2, -1)
    guided = velocity[:, 1] + guidance * (velocity[:, 0] - velocity[:, 1])
    latent_next = latent + euler_step * guided.reshape(latent.shape)
    return (received[None], refreshed[None], latent_next)


def solution(mesh):
    placed = (
        P("section", "blk", None, None),
        P("section", "blk", None, None),
        P("section", "blk", None),
        P("section", None, None, "head"),
        P("section", "head", None),
        P("section", None, "blk", None, None, "head"),
        P("section", "blk", None, None, "head"),
        P("blk"),
        P(),
        P("blk", None, None),
        P(),
        P("blk", "section", None),
    )
    return jax.shard_map(
        shards,
        mesh=mesh,
        in_specs=placed,
        out_specs=(
            P("section", "blk", None, "head"),
            P("section", None, "blk", None, "head"),
            P("blk", "section", None),
        ),
        check_vma=False,
    )
```

profile of v0, /device:TPU:1, one launch (start us, length us, event | category | flops | bytes accessed | tf_op | source)
XLA Modules:
  0.0 173.5 jit_solution(1458555649823151610)
XLA Ops:
  7.2 4.9 %all-to-all-start = ((bf16[8,64,4,2,384]{4,3,2,1,0:T(2,128)(2,1)}), bf16[8,64,4,2,384]{4,3,2,1,0:T(2,128)(2,1)}, u32[]{:S(2)}, u32[]{:S(2)}) async-start(bf16[8,64,4,2,384]{4,3,2,1,0:T(2,128)(2,1)} %bitcast.90), calls=%async_computation | async-start | bytes 6291456 | tf_op jit(solution)/shard_map/all_to_all | solution.py:86
  12.2 0.2 dynamic-slice_reduce_fusion
  12.4 0.1 broadcast_in_dim.32
  12.5 0.1 reshape.238
  12.6 0.1 dynamic_slice.19
  12.6 0.1 iota_compare_fusion.1
  12.7 0.2 tile.9
  13.0 0.3 convert_reduce_fusion
  13.3 0.5 multiply_reduce_fusion
  13.9 6.1 %copy.85 = bf16[1,1536,3,384]{1,3,2,0:T(8,128)(2,1)} copy(bf16[1,1536,3,384]{3,1,2,0:T(8,128)(2,1)} %param.15) | data formatting | bytes 7077888 | tf_op args[3]
  20.0 0.7 add_convert_fusion
  20.6 5.2 %convolution_convert_fusion = bf16[512,1152]{1,0:T(8,128)(2,1)} fusion(bf16[512,1536]{1,0:T(8,128)(2,1)S(1)} %bitcast.95, bf16[1536,1152]{0,1:T(8,128)(2,1)} %bitcast.89), kind=kOutput, calls=%fused_computation.14 | convolution fusion | flops 1812529152 | bytes 6291456 | tf_op jit(solution)/shard_map/dot_general | solution.py:73
  25.9 2.4 %copy.86 = bf16[512,1152]{0,1:T(8,128)(2,1)} copy(bf16[512,1152]{1,0:T(8,128)(2,1)} %convolution_convert_fusion) | data formatting | bytes 2359296 | tf_op jit(solution)/shard_map/convert_element_type | solution.py:77
  28.3 3.7 %reshape.237 = bf16[2,256,3,384]{1,0,3,2:T(2,128)(2,1)} reshape(bf16[512,1152]{0,1:T(8,128)(2,1)} %copy.86) | data formatting | bytes 2359296 | tf_op jit(solution)/shard_map/reshape | solution.py:78
  32.0 2.1 %fusion.35 = (bf16[2,256,1,384]{1,0,3,2:T(2,128)(2,1)S(1)}, bf16[2,256,1,384]{1,0,3,2:T(2,128)(2,1)S(1)}, bf16[2,256,1,384]{1,0,3,2:T(2,128)(2,1)S(1)}) fusion(bf16[2,256,3,384]{1,0,3,2:T(2,128)(2,1)} %reshape.237), kind=kLoop, calls=%fused_computation.71 | loop fusion | bytes 2359296 | tf_op jit(solution)/shard_map/slice | solution.py:81
  34.1 0.8 copy.89
  34.9 1.6 fusion.36
  36.5 2.0 %copy.88 = bf16[2,154,1,384]{1,3,0,2:T(8,128)(2,1)} copy(bf16[2,154,1,384]{3,2,1,0:T(2,128)(2,1)} %get-tuple-element.18) | data formatting | bytes 473088 | tf_op jit(solution)/shard_map/slice | solution.py:96
  38.5 0.8 copy.93
  39.3 2.0 %copy.92 = bf16[2,154,1,384]{1,3,0,2:T(8,128)(2,1)} copy(bf16[2,154,1,384]{3,2,1,0:T(2,128)(2,1)} %get-tuple-element.17) | data formatting | bytes 473088 | tf_op jit(solution)/shard_map/slice | solution.py:118
  41.3 0.1 iota_compare_fusion
  41.4 3.5 %fusion.9 = (f32[2,6,256]{2,1,0:T(8,128)}, f32[2,6,256,154]{2,3,1,0:T(8,128)}) fusion(pred[2,154]{1,0:T(4,128)(4,1)S(1)} %iota_compare_fusion, bf16[2,256,6,64]{1,3,2,0:T(8,128)(2,1)S(1)} %bitcast.86, bf16[2,154,6,64]{1,3,2,0:T(8,128)(2,1)} %bitcast.96), kind=kOutput, calls=%fused_computation.26 | convolution fusion | flops 61971456 | bytes 2534708 | tf_op jit(solution)/shard_map/sqhd,skhd->shqk/dot_general | solution.py:30
  44.9 2.9 %multiply_reduce_fusion.1 = (f32[2,6,256]{2,1,0:T(8,128)}, f32[2,6,256,256]{2,3,1,0:T(8,128)}) fusion(bf16[2,256,6,64]{1,3,2,0:T(8,128)(2,1)S(1)} %bitcast.87, bf16[2,256,6,64]{1,3,2,0:T(8,128)(2,1)S(1)} %bitcast.98), kind=kOutput, calls=%fused_computation.16 | convolution fusion | flops 102233088 | bytes 3944448 | tf_op jit(solution)/shard_map/sqhd,skhd->shqk/dot_general | solution.py:30
  47.8 0.9 all-to-all-done
  48.7 3.4 %copy.90 = bf16[2,4,64,4,2,384]{5,3,2,1,0,4:T(4,128)(2,1)S(1)} copy(bf16[2,4,64,4,2,384]{5,4,3,2,0,1:T(2,128)(2,1)} %bitcast.13) | data formatting | bytes 6291456 | tf_op jit(solution)/shard_map/all_to_all | solution.py:86
  52.1 2.8 %fusion.34 = (bf16[2,256,4,1,384]{4,2,1,0,3:T(4,128)(2,1)}, bf16[2,256,4,1,384]{4,2,1,0,3:T(4,128)(2,1)}) fusion(bf16[2,256,4,2,384]{4,2,1,0,3:T(4,128)(2,1)S(1)} %bitcast.83), kind=kLoop, calls=%fused_computation.70 | loop fusion | bytes 6291456 | tf_op jit(solution)/shard_map/slice | solution.py:89
  54.8 6.0 %reshape_reshape_squeeze.6 = bf16[2,1024,6,64]{3,2,1,0:T(8,128)(2,1)} reshape(bf16[2,256,4,1,384]{4,2,1,0,3:T(4,128)(2,1)} %get-tuple-element.12) | data formatting | bytes 3145728 | tf_op jit(solution)/shard_map/reshape;reshape;squeeze | solution.py:29
  60.9 4.4 %fusion = (f32[2,6,256]{2,1,0:T(8,128)S(1)}, f32[2,6,256,1024]{3,2,1,0:T(8,128)S(1)}) fusion(pred[2,1024]{1,0:T(4,128)(4,1)S(1)} %tile.9, bf16[2,256,6,64]{1,3,2,0:T(8,128)(2,1)S(1)} %bitcast.88, bf16[2,1024,6,64]{3,2,1,0:T(8,128)(2,1)} %reshape_reshape_squeeze.6), kind=kOutput, calls=%fused_computation.3 | convolution fusion | flops 412087296 | bytes 14563328 | tf_op jit(solution)/shard_map/sqhd,skhd->shqk/dot_general | solution.py:30
  65.4 3.3 %fusion.1 = f32[2,6,256]{2,1,0:T(8,128)S(1)} fusion(f32[2,6,256,1024]{3,2,1,0:T(8,128)S(1)} %get-tuple-element.24, f32[2,6,256]{2,1,0:T(8,128)S(1)} %maximum_maximum_fusion, pred[2,1024]{1,0:T(4,128)(4,1)S(1)} %tile.9), kind=kLoop, calls=%fused_computation.4 | loop fusion | flops 12579840 | bytes 12609536 | tf_op jit(solution)/shard_map/reduce_sum | solution.py:112
  68.6 2.0 %copy-done.1 = f32[2,6,256,1024]{3,2,1,0:T(8,128)} copy-done((f32[2,6,256,1024]{3,2,1,0:T(8,128)}, f32[2,6,256,1024]{3,2,1,0:T(8,128)S(1)}, u32[]{:S(2)}) %copy-start.1) | copy-done | bytes 12582936
  70.6 0.5 fusion.6
  71.2 1.0 copy-done.5
  72.2 0.5 fusion.15
  72.7 6.1 %reshape_reshape_squeeze.7 = bf16[2,1024,6,64]{3,2,1,0:T(8,128)(2,1)} reshape(bf16[2,256,4,1,384]{4,2,1,0,3:T(4,128)(2,1)} %get-tuple-element.13) | data formatting | bytes 3145728 | tf_op jit(solution)/shard_map/reshape;reshape;squeeze | solution.py:40
  78.8 2.8 %fusion.16 = f32[2,256,6,64]{1,3,2,0:T(8,128)S(1)} fusion(bf16[2,256,6,64]{1,3,2,0:T(8,128)(2,1)S(1)} %bitcast.101, f32[2,6,256,256]{2,3,1,0:T(8,128)} %get-tuple-element.28, f32[2,6,256]{2,1,0:T(8,128)S(1)} %add_add_fusion, f32[2,6,256]{2,1,0:T(8,128)S(1)} %maximum_maximum_fusion), kind=kOutput, calls=%fused_computation.33 | convolution fusion | flops 103809024 | bytes 4349952 | tf_op jit(solution)/shard_map/shqk,skhd->sqhd/dot_general | solution.py:41
  81.6 2.7 %copy-done.2 = f32[2,6,256,1024]{3,2,1,0:T(8,128)S(1)} copy-done((f32[2,6,256,1024]{3,2,1,0:T(8,128)S(1)}, f32[2,6,256,1024]{3,2,1,0:T(8,128)}, u32[]{:S(2)}) %copy-start.2) | copy-done | bytes 12582936
  84.4 5.7 %fusion.19 = f32[2,256,6,64]{1,3,2,0:T(8,128)S(1)} fusion(bf16[2,1024,6,64]{3,2,1,0:T(8,128)(2,1)} %reshape_reshape_squeeze.7, f32[2,6,256,1024]{3,2,1,0:T(8,128)S(1)} %copy-done.2, f32[2,6,256]{2,1,0:T(8,128)S(1)} %add_add_fusion, f32[2,6,256]{2,1,0:T(8,128)S(1)} %maximum_maximum_fusion, pred[2,1024]{1,0:T(4,128)(4,1)S(1)} %tile.9), kind=kOutput, calls=%fused_computation.37 | convolution fusion | flops 418381824 | bytes 14968832 | tf_op jit(solution)/shard_map/shqk,skhd->sqhd/dot_general | solution.py:41
  90.1 0.7 fusion.22
  90.8 2.2 %convolution_convert_fusion.1 = bf16[2,256,1536]{2,1,0:T(8,128)(2,1)} fusion(bf16[2,256,384]{1,2,0:T(8,128)(2,1)S(1)} %bitcast.99, bf16[1,384,1536]{2,1,0:T(8,128)(2,1)S(1)} %copy-done), kind=kOutput, calls=%fused_computation.15 | convolution fusion | flops 604766208 | bytes 3145728 | tf_op jit(solution)/shard_map/dot_general | solution.py:123
  92.9 4.9 %copy.105 = bf16[2,256,1536]{1,0,2:T(2,128)(2,1)} copy(bf16[2,256,1536]{2,1,0:T(8,128)(2,1)} %convolution_convert_fusion.1) | data formatting | bytes 3145728
  97.8 3.0 %copy.111 = bf16[192,8,2,256]{3,1,2,0:T(8,128)(2,1)} copy(bf16[192,8,2,256]{3,2,1,0:T(2,128)(2,1)} %bitcast.85) | data formatting | bytes 3145728
  100.8 2.9 %copy.97 = bf16[2,256,2,384]{3,2,0,1:T(2,128)(2,1)} copy(bf16[2,256,2,384]{1,0,3,2:T(2,128)(2,1)S(1)} %slice-done) | data formatting | bytes 1572864 | tf_op jit(solution)/shard_map/stack | solution.py:82
  103.7 3.6 %all-to-all-start.1 = ((bf16[2,256,2,384]{3,2,0,1:T(2,128)(2,1)}), bf16[2,256,2,384]{3,2,0,1:T(2,128)(2,1)S(1)}, u32[]{:S(2)}, u32[]{:S(2)}) async-start(bf16[2,256,2,384]{3,2,0,1:T(2,128)(2,1)} %copy.97), calls=%async_computation.1 | async-start | bytes 1572864 | tf_op jit(solution)/shard_map/all_to_all | solution.py:83
  107.4 2.1 %convert_element_type.70 = f32[1,2,256,1536]{3,2,1,0:T(8,128)} convert(bf16[1,2,256,1536]{3,2,1,0:T(8,128)(2,1)S(1)} %copy-done.3) | non-fusion elementwise | flops 786432 | bytes 4718592 | tf_op jit(solution)/shard_map/convert_element_type | solution.py:67
  109.4 0.7 convert_bitcast_fusion
  110.2 27.5 %reduce-scatter.4.cloned.1.call-done = bf16[384,512]{1,0:T(8,128)(2,1)} async-done(((bf16[1536,512]{1,0:T(8,128)(2,1)}), bf16[384,512]{1,0:T(8,128)(2,1)}) %reduce-scatter.4.cloned.1.call-update) | async-done | bytes 393232
  137.6 1.1 reshape.244
  138.7 0.7 copy.106
  139.4 2.0 %fusion.28 = bf16[2,256,384]{2,1,0:T(8,128)(2,1)} fusion(bf16[2,256,384]{2,1,0:T(8,128)(2,1)S(1)} %copy.106, f32[1,2,256,1536]{3,2,1,0:T(8,128)} %convert_element_type.70, s32[]{:T(128)S(6)} %select_n.30, f32[2,384]{1,0:T(2,128)S(1)} %convert_bitcast_fusion), kind=kLoop, calls=%fused_computation.45 | loop fusion | flops 786432 | bytes 1575940 | tf_op jit(solution)/shard_map/convert_element_type | solution.py:140
  141.4 0.8 collective-permute-start
  142.3 0.6 copy_bitcast_fusion
  142.9 0.1 copy.98
  143.0 0.1 copy.99
  143.1 1.7 copy.101
  144.8 1.1 dynamic-slice_select_fusion
  145.9 16.9 %all_gather.3 = bf16[2,128,1536]{2,1,0:T(8,128)(2,1)S(1)} all-gather(bf16[2,128,384]{2,1,0:T(8,128)(2,1)S(1)} %dynamic-slice_select_fusion), channel_id=1, replica_groups=mesh['section'=2,'head'=4,'blk'=4] {'head'}, dimensions={2}, use_global_device_ids=true | all-gather | bytes 983040 | tf_op jit(solution)/shard_map/all_gather | solution.py:144
  162.7 0.2 convert_reduce_fusion.1
  162.9 0.3 fusion.10
  163.3 0.4 fusion.13
  163.7 0.3 fusion.38
  164.0 0.1 reshape.240
  164.2 0.1 fusion.37
  164.2 0.6 multiply_add_fusion
  164.8 1.8 %copy.125 = bf16[1,2,256,384]{3,2,1,0:T(8,128)(2,1)} copy(bf16[1,2,256,384]{3,2,1,0:T(8,128)(2,1)} %bitcast.23) | data formatting | bytes 786432
  (57 shorter events, 0.4 us)
Async XLA Ops:
  7.2 83.6 %copy-start = (bf16[1,384,1536]{2,1,0:T(8,128)(2,1)S(1)}, bf16[1,384,1536]{2,1,0:T(8,128)(2,1)}, u32[]{:S(2)}) copy-start(bf16[1,384,1536]{2,1,0:T(8,128)(2,1)} %param.16) | copy-start | bytes 3538948
  7.2 5.0 %copy-start.18 = (s32[4,4]{1,0:T(4,128)S(1)}, s32[4,4]{1,0:T(4,128)}, u32[]{:S(2)}) copy-start(s32[4,4]{1,0:T(4,128)} %param.20) | copy-start | bytes 196
  7.2 5.8 %copy-start.17 = (bf16[1,2,2,1536]{3,2,1,0:T(2,128)(2,1)S(1)}, bf16[1,2,2,1536]{3,2,1,0:T(2,128)(2,1)}, u32[]{:S(2)}) copy-start(bf16[1,2,2,1536]{3,2,1,0:T(2,128)(2,1)} %param.13) | copy-start | bytes 36868
  7.2 5.8 %copy-start.3 = (bf16[1,2,256,1536]{3,2,1,0:T(8,128)(2,1)S(1)}, bf16[1,2,256,1536]{3,2,1,0:T(8,128)(2,1)}, u32[]{:S(2)}) copy-start(bf16[1,2,256,1536]{3,2,1,0:T(8,128)(2,1)} %param.12) | copy-start | bytes 4718596
  7.2 41.4 %all-to-all-start = ((bf16[8,64,4,2,384]{4,3,2,1,0:T(2,128)(2,1)}), bf16[8,64,4,2,384]{4,3,2,1,0:T(2,128)(2,1)}, u32[]{:S(2)}, u32[]{:S(2)}) async-start(bf16[8,64,4,2,384]{4,3,2,1,0:T(2,128)(2,1)} %bitcast.90), calls=%async_computation | async-start | bytes 6291456 | tf_op jit(solution)/shard_map/all_to_all | solution.py:86
  12.1 125.5 %reduce-scatter.4.cloned.1.call-start = ((), (), s32[]{:S(2)}) async-start(), calls=%async_computation.3 | async-start | bytes 1966080
  32.0 3.0 %copy-start.7 = (bf16[1,2,154,2,384]{4,3,2,1,0:T(2,128)(2,1)S(1)}, bf16[1,2,154,2,384]{4,3,2,1,0:T(2,128)(2,1)}, u32[]{:S(2)}) copy-start(bf16[1,2,154,2,384]{4,3,2,1,0:T(2,128)(2,1)} %param.18) | copy-start | bytes 1419268
  34.1 7.3 %copy-start.19 = (s32[2]{0:T(128)S(1)}, s32[2]{0:T(128)}, u32[]{:S(2)}) copy-start(s32[2]{0:T(128)} %param.19) | copy-start | bytes 28
  39.3 5.6 %copy-start.8 = (bf16[2,256,1,384]{1,3,0,2:T(8,128)(2,1)S(1)}, bf16[2,256,1,384]{1,3,0,2:T(8,128)(2,1)}, u32[]{:S(2)}) copy-start(bf16[2,256,1,384]{1,3,0,2:T(8,128)(2,1)} %copy.89) | copy-start | bytes 1179652
  60.9 4.5 %copy-start.12 = (f32[2,6,256]{2,1,0:T(8,128)S(1)}, f32[2,6,256]{2,1,0:T(8,128)}, u32[]{:S(2)}) copy-start(f32[2,6,256]{2,1,0:T(8,128)} %get-tuple-element.25) | copy-start | bytes 36868
  60.9 4.5 %copy-start.13 = (f32[2,6,256]{2,1,0:T(8,128)S(1)}, f32[2,6,256]{2,1,0:T(8,128)}, u32[]{:S(2)}) copy-start(f32[2,6,256]{2,1,0:T(8,128)} %get-tuple-element.27) | copy-start | bytes 36868
  65.3 5.3 %copy-start.1 = (f32[2,6,256,1024]{3,2,1,0:T(8,128)}, f32[2,6,256,1024]{3,2,1,0:T(8,128)S(1)}, u32[]{:S(2)}) copy-start(f32[2,6,256,1024]{3,2,1,0:T(8,128)S(1)} %get-tuple-element.24) | copy-start | bytes 37748740
  65.4 5.3 %copy-start.4 = (f32[2,6,256,256]{2,3,1,0:T(8,128)S(1)}, f32[2,6,256,256]{2,3,1,0:T(8,128)}, u32[]{:S(2)}) copy-start(f32[2,6,256,256]{2,3,1,0:T(8,128)} %get-tuple-element.28) | copy-start | bytes 9437188
  70.6 1.5 copy-start.5
  72.7 6.2 %copy-start.10 = (bf16[2,256,1,384]{1,3,0,2:T(8,128)(2,1)S(1)}, bf16[2,256,1,384]{1,3,0,2:T(8,128)(2,1)}, u32[]{:S(2)}) copy-start(bf16[2,256,1,384]{1,3,0,2:T(8,128)(2,1)} %copy.93) | copy-start | bytes 1179652
  78.8 5.5 %copy-start.2 = (f32[2,6,256,1024]{3,2,1,0:T(8,128)S(1)}, f32[2,6,256,1024]{3,2,1,0:T(8,128)}, u32[]{:S(2)}) copy-start(f32[2,6,256,1024]{3,2,1,0:T(8,128)} %copy-done.1) | copy-start | bytes 37748740
  84.4 5.7 %copy-start.6 = (f32[2,6,256,154]{2,3,1,0:T(8,128)S(1)}, f32[2,6,256,154]{2,3,1,0:T(8,128)}, u32[]{:S(2)}) copy-start(f32[2,6,256,154]{2,3,1,0:T(8,128)} %get-tuple-element.26) | copy-start | bytes 5677060
  84.4 5.7 %copy-start.9 = (bf16[2,154,1,384]{1,3,0,2:T(8,128)(2,1)S(1)}, bf16[2,154,1,384]{1,3,0,2:T(8,128)(2,1)}, u32[]{:S(2)}) copy-start(bf16[2,154,1,384]{1,3,0,2:T(8,128)(2,1)} %copy.92) | copy-start | bytes 709636
  97.8 3.0 %slice-start = ((bf16[2,256,3,384]{1,0,3,2:T(2,128)(2,1)}), bf16[2,256,2,384]{1,0,3,2:T(2,128)(2,1)S(1)}, s32[]{:S(2)}) async-start(bf16[2,256,3,384]{1,0,3,2:T(2,128)(2,1)} %reshape.237), calls=%async_computation.4 | async-start | bytes 1572864 | tf_op jit(solution)/shard_map/stack | solution.py:82
  103.7 5.7 %copy-start.15 = (bf16[2,2,1536]{2,1,0:T(2,128)(2,1)S(1)}, bf16[2,2,1536]{2,1,0:T(2,128)(2,1)}, u32[]{:S(2)}) copy-start(bf16[2,2,1536]{2,1,0:T(2,128)(2,1)} %param.21) | copy-start | bytes 36868
  103.7 39.1 %all-to-all-start.1 = ((bf16[2,256,2,384]{3,2,0,1:T(2,128)(2,1)}), bf16[2,256,2,384]{3,2,0,1:T(2,128)(2,1)S(1)}, u32[]{:S(2)}, u32[]{:S(2)}) async-start(bf16[2,256,2,384]{3,2,0,1:T(2,128)(2,1)} %copy.97), calls=%async_computation.1 | async-start | bytes 1572864 | tf_op jit(solution)/shard_map/all_to_all | solution.py:83
  141.4 3.4 %collective-permute-start = (bf16[2,256,384]{2,1,0:T(8,128)(2,1)}, bf16[2,256,384]{2,1,0:T(8,128)(2,1)}, u32[]{:S(2)}, u32[]{:S(2)}) collective-permute-start(bf16[2,256,384]{2,1,0:T(8,128)(2,1)} %fusion.28), channel_id=1, source_target_pairs={{0,16},{16,0},{1,17},{17,1},{2,18},{18,2},{3,19},{19,3},{4,20},{20... | collective-permute-start | bytes 1179656 | tf_op jit(solution)/shard_map/ppermute | solution.py:16
  143.0 20.3 %copy-start.14 = (f32[2,1536]{1,0:T(2,128)S(1)}, f32[2,1536]{1,0:T(2,128)}, u32[]{:S(2)}) copy-start(f32[2,1536]{1,0:T(2,128)} %get-tuple-element.32) | copy-start | bytes 36868
  143.1 20.6 %copy-start.11 = (bf16[1536,64]{0,1:T(8,128)(2,1)S(1)}, bf16[1536,64]{0,1:T(8,128)(2,1)}, u32[]{:S(2)}) copy-start(bf16[1536,64]{0,1:T(8,128)(2,1)} %param.22) | copy-start | bytes 589828
  144.8 19.4 %copy-start.16 = (f32[1,64,128]{2,1,0:T(8,128)S(1)}, f32[1,64,128]{2,1,0:T(8,128)}, u32[]{:S(2)}) copy-start(f32[1,64,128]{2,1,0:T(8,128)} %param.23) | copy-start | bytes 98308
Sparse Core Ops, SparseCore 0:
  100.9 36.6 reduce-scatter.3
where the time goes:
time: 176 us; the launch traced here: 173 us
  local copies, waits for them, and re-layouts  63.3 us (36%)
  waiting for transfers between devices  28.4 us (16%)
  matrix products  27.7 us (16%)
  blocking collectives  16.9 us (10%)
  between operations  14.5 us (8%)
  other arithmetic  13.4 us (8%)
  starting transfers between devices  9.43 us (5%)
    unnamed x2, waiting for transfers between devices  27.5 us
    unnamed x49, local copies, waits for them, and re-layouts  25.6 us
    all_gather x1, blocking collectives, shards(): final_rows = lax.all_gather(last_half, 'head', axis=2, tiled=True)  16.9 us
    dot_general x3, matrix products, piece_scores(): jnp.einsum('sqhd,skhd->shqk', query_heads, key_heads, preferred_element_t...  10.8 us
    dot_general x3, matrix products, piece_values(): jnp.einsum('shqk,skhd->sqhd', probs_piece, value_heads, preferred_element...  9.17 us
    another operation x1, local copies, waits for them, and re-layouts, piece_values(): value_heads = value_piece.reshape(seq_dev, -1, head_count, HEAD_DIM)  6.13 us
    another operation x1, local copies, waits for them, and re-layouts, piece_scores(): key_heads = key_piece.reshape(seq_dev, -1, head_count, HEAD_DIM)  6.03 us
    dot_general x1, matrix products, shards(): jnp.dot(normed.reshape(seq_dev * patch_rows, model_width), qkv_weight[0]....  5.23 us
  transfers between devices with their start and end apart: 4, of which 2 were waited for; matrix products, arithmetic and copies ran while one was open for 27% of the time, Pallas kernels for 0%

commit v1 on v0

v1 whole, which is shorter than its diff:
```python
import functools
import jax
import jax.numpy as jnp
from jax import lax
from jax.experimental import pallas as pl
from jax.experimental.pallas import tpu as pltpu
from jax.sharding import PartitionSpec as P

HEAD_DIM = 64
LANES = 128
TEXT_PAD = 256
norm_eps = 1e-06
guidance = 4.0
euler_step = -0.25
F32 = jnp.float32
BF16 = jnp.bfloat16
NT = (((1,), (1,)), ((), ()))


def dot(a, b):
    return jnp.dot(a, b, preferred_element_type=F32)


def kernel(
    n_blk, n_head, piece, rows,
    x_ref, mod_ref, gate_ref, wqkv_ref, wout_ref, stale_ref, text_ref, bias_ref,
    fmod_ref, fw_ref, latent_ref,
    recv_ref, fresh_out_ref, latent_out_ref,
    kv, queries, fresh, attended, part_send, part_land, own_out, vel_own, vel_land, guided_ref,
    stale_send, stale_recv, own_sem, fresh_send, fresh_recv, fresh_own,
    part_ssem, part_rsem, sec_ssem, sec_rsem, vel_ssem, vel_rsem,
):
    sec = lax.axis_index("section")
    head = lax.axis_index("head")
    blk = lax.axis_index("blk")
    seqs, tokens, width = x_ref.shape
    group = wqkv_ref.shape[2]
    base = TEXT_PAD + tokens
    half = tokens // 2

    barrier = pltpu.get_barrier_semaphore()
    for d in range(1, n_blk):
        pl.semaphore_signal(barrier, inc=1, device_id={"blk": lax.rem(blk + d, n_blk)})
    for d in range(1, n_head):
        pl.semaphore_signal(barrier, inc=1, device_id={"head": lax.rem(head + d, n_head)})
    pl.semaphore_signal(barrier, inc=1, device_id={"section": 1 - sec})
    pl.semaphore_wait(barrier, n_blk - 1 + n_head - 1 + 1)

    def place(src):
        return pl.ds(pl.multiple_of(base + src * piece, 16), piece)

    stale_copies = []
    for s in range(seqs):
        for d in range(1, n_blk):
            dst = lax.rem(blk + d, n_blk)
            copy = pltpu.make_async_remote_copy(
                src_ref=stale_ref.at[dst * seqs + s],
                dst_ref=kv.at[s, :, place(blk), :],
                send_sem=stale_send.at[s, d - 1],
                recv_sem=stale_recv.at[s, d - 1],
                device_id={"blk": dst},
            )
            copy.start()
            stale_copies.append(copy)
    own_copies = []
    for s in range(seqs):
        copy = pltpu.make_async_copy(
            stale_ref.at[blk * seqs + s], kv.at[s, :, place(blk), :], own_sem.at[s]
        )
        copy.start()
        own_copies.append(copy)

    for s in range(seqs):
        x = x_ref[s].astype(F32)
        mean = jnp.mean(x, axis=-1, keepdims=True)
        centered = x - mean
        var = jnp.mean(centered * centered, axis=-1, keepdims=True)
        inv = 1.0 / jnp.sqrt(var + norm_eps)
        normed = (centered * inv * (1.0 + mod_ref[s, 1:2, :]) + mod_ref[s, 0:1, :]).astype(BF16)
        queries[s] = (dot(normed, wqkv_ref[0]).astype(BF16) * 0.125).astype(BF16)
        for j in range(2):
            new = dot(normed, wqkv_ref[j + 1]).astype(BF16)
            kv[s, j, 0:TEXT_PAD, :] = text_ref[s, j]
            kv[s, j, TEXT_PAD:base, :] = new
            fresh[s, j] = new.astype(fresh.dtype)

    def fresh_rows(dst):
        return pl.ds(pl.multiple_of(dst * rows, 8), rows)

    fresh_copies = []
    for d in range(1, n_blk):
        dst = lax.rem(blk + d, n_blk)
        copy = pltpu.make_async_remote_copy(
            src_ref=fresh.at[:, :, fresh_rows(dst), :],
            dst_ref=fresh_out_ref.at[pl.ds(blk * seqs, seqs)],
            send_sem=fresh_send.at[d - 1],
            recv_sem=fresh_recv.at[d - 1],
            device_id={"blk": dst},
        )
        copy.start()
        fresh_copies.append(copy)
    own_fresh = pltpu.make_async_copy(
        fresh.at[:, :, fresh_rows(blk), :], fresh_out_ref.at[pl.ds(blk * seqs, seqs)], fresh_own
    )
    own_fresh.start()

    shift_term, scale_terms = [], []
    for s in range(seqs):
        lhs = jnp.broadcast_to(fmod_ref[s, 0:1, :], (8, width)).astype(BF16)
        shift_term.append(
            lax.dot_general(lhs, fw_ref[s], NT, preferred_element_type=F32)[0:1]
        )
        terms = []
        for g in range(n_head):
            cut = slice(g * group, (g + 1) * group)
            wide = jnp.broadcast_to(1.0 + fmod_ref[s, 1:2, cut], (8, group))
            high = wide.astype(BF16)
            low = (wide - high.astype(F32)).astype(BF16)
            w = fw_ref[s, :, cut]
            terms.append(
                (
                    lax.dot_general(high, w, NT, preferred_element_type=F32)
                    + lax.dot_general(low, w, NT, preferred_element_type=F32)
                )[0:1]
            )
        scale_terms.append(terms)

    lane = lax.broadcasted_iota(jnp.int32, (1, LANES), 1)
    low_half = lane < HEAD_DIM
    share = pl.ds(pl.multiple_of(head * group, LANES), group)
    part_copies = []
    for s in range(seqs):
        own_copies[s].wait()
        for d in range(1, n_blk):
            stale_copies[s * (n_blk - 1) + d - 1].wait_recv()
        bias = bias_ref[s]
        for p in range(group // LANES):
            cut = slice(p * LANES, (p + 1) * LANES)
            q = queries[s, :, cut]
            k = kv[s, 0, :, cut]
            v = kv[s, 1, :, cut]
            outs = []
            for side in (low_half, jnp.logical_not(low_half)):
                q_side = q * side.astype(BF16)
                scores = lax.dot_general(q_side, k, NT, preferred_element_type=F32) + bias
                top = jnp.max(scores, axis=-1, keepdims=True)
                weights = jnp.exp(scores - top)
                total = jnp.sum(weights, axis=-1, keepdims=True)
                outs.append(dot(weights.astype(BF16), v) / total)
            attended[s, :, cut] = jnp.where(low_half, outs[0], outs[1]).astype(BF16)
        att = attended[s]
        for g in range(n_head):
            part_send[s, g] = dot(att, wout_ref[:, g * group : (g + 1) * group]).astype(BF16)
        for d in range(1, n_head):
            dst = lax.rem(head + d, n_head)
            copy = pltpu.make_async_remote_copy(
                src_ref=part_send.at[s, dst],
                dst_ref=part_land.at[s, d - 1],
                send_sem=part_ssem.at[s, d - 1],
                recv_sem=part_rsem.at[s, d - 1],
                device_id={"head": dst},
            )
            copy.start()
            part_copies.append(copy)

    sec_copies = []
    for s in range(seqs):
        total = part_send[s, head].astype(F32)
        for d in range(1, n_head):
            part_copies[s * (n_head - 1) + d - 1].wait_recv()
            total = total + part_land[s, d - 1].astype(F32)
        own_out[s] = (x_ref[s, :, share].astype(F32) + gate_ref[s, :, share] * total).astype(BF16)
        copy = pltpu.make_async_remote_copy(
            src_ref=own_out.at[s],
            dst_ref=recv_ref.at[s],
            send_sem=sec_ssem.at[s],
            recv_sem=sec_rsem.at[s],
            device_id={"section": 1 - sec},
        )
        copy.start()
        sec_copies.append(copy)

    wide_lane = lax.broadcasted_iota(jnp.int32, (half, LANES), 1)
    stats = jnp.zeros((half, LANES), F32)
    product = jnp.zeros((half, LANES), F32)
    first = sec == 0
    for s in range(seqs):
        sec_copies[s].wait_recv()
        x = jnp.where(
            first, recv_ref[s, 0:half].astype(F32), own_out[s, half:tokens].astype(F32)
        )
        mean = jnp.mean(x, axis=-1, keepdims=True)
        centered = x - mean
        squares = jnp.sum(centered * centered, axis=-1, keepdims=True)
        scaled = (centered * (1.0 + fmod_ref[s, 1:2, share])).astype(BF16)
        product = product + lax.dot_general(
            scaled, fw_ref[s, :, share], NT, preferred_element_type=F32
        )
        stats = jnp.where(wide_lane == 2 * s, mean, stats)
        stats = jnp.where(wide_lane == 2 * s + 1, squares, stats)
    vel_own[:, 0:LANES] = product
    vel_own[:, LANES : 2 * LANES] = stats
    vel_copies = []
    for d in range(1, n_head):
        copy = pltpu.make_async_remote_copy(
            src_ref=vel_own,
            dst_ref=vel_land.at[head],
            send_sem=vel_ssem.at[d - 1],
            recv_sem=vel_rsem.at[d - 1],
            device_id={"head": lax.rem(head + d, n_head)},
        )
        copy.start()
        vel_copies.append(copy)
    for copy in vel_copies:
        copy.wait_recv()
    vel_land[head] = vel_own[...]
    velocity = jnp.zeros((half, LANES), F32)
    summed = vel_land[0, :, 0:LANES]
    for g in range(1, n_head):
        summed = summed + vel_land[g, :, 0:LANES]
    for s in range(seqs):
        means = [vel_land[g, :, LANES + 2 * s : LANES + 2 * s + 1] for g in range(n_head)]
        mean = sum(means) / n_head
        var = sum(
            vel_land[g, :, LANES + 2 * s + 1 : LANES + 2 * s + 2]
            + group * (means[g] - mean) * (means[g] - mean)
            for g in range(n_head)
        ) / width
        inv = 1.0 / jnp.sqrt(var + norm_eps)
        mine = low_half if s == 0 else jnp.logical_not(low_half)
        corrected = jnp.where(mine, summed, 0.0)
        for g in range(n_head):
            corrected = corrected + (means[g] - mean) * scale_terms[s][g]
        velocity = velocity + corrected * inv + shift_term[s]
    weighted = velocity * jnp.where(low_half, guidance, 1.0 - guidance)
    guided_ref[...] = weighted + pltpu.roll(weighted, HEAD_DIM, 1)
    even = guided_ref[pl.ds(0, half // 2, 2), :]
    odd = guided_ref[pl.ds(1, half // 2, 2), :]
    latent_out_ref[...] = latent_ref[...] + euler_step * jnp.where(low_half, even, odd)

    own_fresh.wait()
    for copy in fresh_copies:
        copy.wait()
    for copy in stale_copies + part_copies + sec_copies + vel_copies:
        copy.wait_send()


def shards(
    n_blk, n_head,
    section_input, modulation, attn_gate, qkv_weight, out_weight, kv_cache, text_kv,
    text_len, patch_order, final_mod, final_weight, latent,
):
    section_index = lax.axis_index("section")
    own_order = lax.dynamic_index_in_dim(patch_order, section_index, 1, keepdims=False)
    seq_patch = jnp.repeat(own_order, 2)
    x = section_input[0]
    seqs, tokens, width = x.shape
    group = qkv_weight.shape[3]
    cache = kv_cache[0]
    all_seqs, rows, patches = cache.shape[:3]
    kept = (patches - 1) * rows
    piece = -(-kept // 16) * 16
    at = seq_patch[:, None, None, None, None]
    stale = jnp.stack(
        [
            jnp.where(j < at[:, :, 0], cache[:, :, j], cache[:, :, j + 1])
            for j in range(patches - 1)
        ],
        axis=1,
    )
    stale = stale.transpose(0, 3, 1, 2, 4).reshape(all_seqs, 2, kept, group)
    stale = jnp.pad(stale, ((0, 0), (0, 0), (0, piece - kept), (0, 0)))
    text_count = text_kv.shape[2]
    text = jnp.pad(
        text_kv[0].transpose(0, 2, 1, 3), ((0, 0), (0, 0), (0, TEXT_PAD - text_count), (0, 0))
    )
    base = TEXT_PAD + tokens
    keys = base + n_blk * piece
    position = jnp.arange(keys, dtype=jnp.int32)[None, :]
    counted = jnp.where(
        position < base,
        (position >= TEXT_PAD) | (position < text_len[:, None]),
        (position - base) % piece < kept,
    )
    bias = jnp.where(counted, 0.0, -1e30).astype(F32)[:, None, :]
    weight_t = final_weight.T
    out_ch = weight_t.shape[0]
    final_t = jnp.stack(
        [jnp.pad(weight_t, ((0, out_ch), (0, 0))), jnp.pad(weight_t, ((out_ch, 0), (0, 0)))]
    )
    fresh_type = BF16 if rows % 16 == 0 else F32
    half = tokens // 2
    vmem = pl.BlockSpec(memory_space=pltpu.VMEM)
    dma = pltpu.SemaphoreType.DMA
    received, fresh, latent_next = pl.pallas_call(
        functools.partial(kernel, n_blk, n_head, piece, rows),
        out_shape=(
            jax.ShapeDtypeStruct((seqs, tokens, group), BF16),
            jax.ShapeDtypeStruct((all_seqs, 2, rows, group), fresh_type),
            jax.ShapeDtypeStruct(latent.shape[1:], F32),
        ),
        in_specs=[vmem] * 5 + [pl.BlockSpec(memory_space=pl.ANY)] + [vmem] * 5,
        out_specs=(vmem, vmem, vmem),
        scratch_shapes=[
            pltpu.VMEM((seqs, 2, keys, group), BF16),
            pltpu.VMEM((seqs, tokens, group), BF16),
            pltpu.VMEM((seqs, 2, tokens, group), fresh_type),
            pltpu.VMEM((seqs, tokens, group), BF16),
            pltpu.VMEM((seqs, n_head, tokens, group), BF16),
            pltpu.VMEM((seqs, n_head - 1, tokens, group), BF16),
            pltpu.VMEM((seqs, tokens, group), BF16),
            pltpu.VMEM((half, 2 * LANES), F32),
            pltpu.VMEM((n_head, half, 2 * LANES), F32),
            pltpu.VMEM((half, LANES), F32),
            dma((seqs, n_blk - 1)),
            dma((seqs, n_blk - 1)),
            dma((seqs,)),
            dma((n_blk - 1,)),
            dma((n_blk - 1,)),
            dma(()),
            dma((seqs, n_head - 1)),
            dma((seqs, n_head - 1)),
            dma((seqs,)),
            dma((seqs,)),
            dma((n_head - 1,)),
            dma((n_head - 1,)),
        ],
        compiler_params=pltpu.CompilerParams(
            collective_id=0, has_side_effects=True, vmem_limit_bytes=56 * 1024 * 1024
        ),
    )(
        x,
        modulation[0].astype(F32),
        attn_gate[0].astype(F32)[:, None, :],
        qkv_weight[0].transpose(1, 0, 2),
        out_weight[0],
        stale,
        text,
        bias,
        final_mod.astype(F32),
        final_t,
        latent[0],
    )
    cache_patch = fresh.astype(BF16).transpose(0, 2, 1, 3)
    return (received[None], cache_patch[None], latent_next[None])


def solution(mesh):
    placed = (
        P("section", "blk", None, None),
        P("section", "blk", None, None),
        P("section", "blk", None),
        P("section", None, None, "head"),
        P("section", "head", None),
        P("section", None, "blk", None, None, "head"),
        P("section", "blk", None, None, "head"),
        P("blk"),
        P(),
        P("blk", None, None),
        P(),
        P("blk", "section", None),
    )
    return jax.shard_map(
        functools.partial(shards, mesh.shape["blk"], mesh.shape["head"]),
        mesh=mesh,
        in_specs=placed,
        out_specs=(
            P("section", "blk", None, "head"),
            P("section", None, "blk", None, "head"),
            P("blk", "section", None),
        ),
        check_vma=False,
    )
```

time: 176 us -> 97.8 us (0.56)
  the two profiles are of different devices: /device:TPU:1 before, /device:TPU:29 now
where the time goes in v1:
time: 97.8 us; the launch traced here: 97.6 us
  Pallas kernels  76.1 us (78%)
  other arithmetic  12 us (12%)
  local copies, waits for them, and re-layouts  8.75 us (9%)
    pallas_call x1, Pallas kernels, shards(): pl.pallas_call(functools.partial(kernel, n_blk, n_head, piece, rows), out...  76.1 us
    unnamed x18, local copies, waits for them, and re-layouts  5.32 us
    transpose x1, other arithmetic, shards(): stale = stale.transpose(0, 3, 1, 2, 4).reshape(all_seqs, 2, kept, group)  4.02 us
    select_n x1, other arithmetic, shards(): jnp.where(j < at[:, :, 0], cache[:, :, j], cache[:, :, j + 1])  3.54 us

profile of v1, /device:TPU:29, one launch (start us, length us, event | category | flops | bytes accessed | tf_op | source)
XLA Modules:
  0.0 97.6 jit_solution(2894270053707917854)
XLA Ops:
  0.6 0.9 compare_reduce_fusion.2
  1.5 0.1 broadcast_in_dim.62
  1.6 0.1 gt.47
  1.7 0.1 broadcast_in_dim.64
  1.8 0.1 gt.50
  1.9 0.1 broadcast_in_dim.66
  1.9 0.1 gt.53
  2.0 3.5 %broadcast_select_fusion.2 = (bf16[8,1,64,2,384]{4,3,2,0,1:T(2,128)(2,1)S(1)}, bf16[8,1,64,2,384]{4,3,2,0,1:T(2,128)(2,1)S(1)}, bf16[8,1,64,2,384]{4,3,2,0,1:T(2,128)(2,1)S(1)}) fusion(pred[8]{0:T(512)(128)(4,1)S(1)} %gt.47, bf16[8,64,4,2,384]{4,3,2,1,0:T(2,128)(2,1)} %bitcast.59, pred[8]{0:T(512)(128)(4,1)S(1)} %gt.53, pred[8]{0:T(512)(128)(4,1)S(1)} %gt.50), kind=kLoop, calls=%fused_computation.3 | loop fusion | flops 1179648 | bytes 5505048 | tf_op jit(solution)/shard_map/jit(_where)/select_n | solution.py:266
  5.6 4.0 %maximum_bitcast_fusion = bf16[8,2,3,64,384]{4,1,3,0,2:T(2,128)(2,1)S(1)} fusion(bf16[8,1,64,2,384]{4,3,2,0,1:T(2,128)(2,1)S(1)} %get-tuple-element.16, bf16[8,1,64,2,384]{4,3,2,0,1:T(2,128)(2,1)S(1)} %get-tuple-element.17, bf16[8,1,64,2,384]{4,3,2,0,1:T(2,128)(2,1)S(1)} %get-tuple-element.15), kind=kLoop, calls=%fused_computation | loop fusion | flops 2359296 | bytes 4718592 | tf_op jit(solution)/shard_map/transpose | solution.py:271
  9.6 0.0 copy-start.1
  9.6 1.9 %copy.19 = bf16[8,2,3,64,384]{4,3,2,1,0:T(8,128)(2,1)} copy(bf16[8,2,3,64,384]{4,1,3,0,2:T(2,128)(2,1)S(1)} %maximum_bitcast_fusion) | data formatting | bytes 4718592 | tf_op jit(solution)/shard_map/transpose | solution.py:271
  11.5 0.0 copy-start.6
  11.5 0.0 copy-start
  11.5 0.0 copy-done.1
  11.6 0.0 copy-start.3
  11.6 0.0 copy-start.4
  11.6 0.0 copy-start.5
  11.6 0.1 pad_bitcast_fusion.1
  11.6 1.0 pad_maximum_fusion.fw_ref
  12.6 0.0 copy-done.6
  12.6 0.7 select_select_fusion.bias_ref
  13.3 0.0 copy-done
  13.3 0.1 copy.27
  13.4 1.0 pad.12.text_ref
  14.3 0.0 copy-done.3
  14.3 0.6 bitcast_convert_fusion.1.mod_ref
  15.0 0.0 copy-done.4
  15.0 0.6 convert_element_type.31.fmod_ref
  15.6 0.0 copy-done.5
  15.6 0.6 bitcast_convert_fusion.gate_ref
  16.2 76.1 %shard_map.139 = (bf16[2,256,384]{2,1,0:T(8,128)(2,1)}, bf16[8,2,64,384]{3,2,1,0:T(8,128)(2,1)}, f32[64,128]{1,0:T(8,128)}) custom-call(bf16[2,256,1536]{2,1,0:T(8,128)(2,1)} %bitcast.61, f32[2,2,1536]{2,1,0:T(2,128)} %bitcast_convert_fusion.1.mod_ref, f32[2,1,1536]{2,1,0:T(1,128)} %bitcast_convert_fusion.gate_ref, bf16[3,1536,384]{2,1,0:T(8,128)(2,1)} %bitcast.58, ...), custom_call_target="tpu_custom_call" | custom-call | tf_op jit(solution)/shard_map/pallas_call | solution.py:295
  92.3 0.0 copy-start.2
  92.4 2.8 %copy.21 = bf16[1,8,64,2,384]{4,3,2,1,0:T(2,128)(2,1)} copy(bf16[1,8,64,2,384]{4,2,3,1,0:T(8,128)(2,1)} %bitcast.63) | data formatting | bytes 1572864
  95.2 1.8 %copy.30 = bf16[1,2,256,384]{3,2,1,0:T(8,128)(2,1)} copy(bf16[1,2,256,384]{3,2,1,0:T(8,128)(2,1)} %bitcast.64) | data formatting | bytes 786432
  97.0 0.0 copy-done.2
  97.0 0.6 copy.31
  (2 shorter events, 0.0 us)
Async XLA Ops:
  9.6 2.0 %copy-start.1 = (bf16[1536,64]{0,1:T(8,128)(2,1)S(1)}, bf16[1536,64]{0,1:T(8,128)(2,1)}, u32[]{:S(2)}) copy-start(bf16[1536,64]{0,1:T(8,128)(2,1)} %param.22) | copy-start | bytes 589828
  11.5 1.1 %copy-start.6 = (s32[2]{0:T(128)S(1)}, s32[2]{0:T(128)}, u32[]{:S(2)}) copy-start(s32[2]{0:T(128)} %param.19) | copy-start | bytes 28
  11.5 1.8 %copy-start = (bf16[1,2,154,2,384]{4,3,2,1,0:T(2,128)(2,1)S(1)}, bf16[1,2,154,2,384]{4,3,2,1,0:T(2,128)(2,1)}, u32[]{:S(2)}) copy-start(bf16[1,2,154,2,384]{4,3,2,1,0:T(2,128)(2,1)} %param.18) | copy-start | bytes 1419268
  11.6 2.8 %copy-start.3 = (bf16[1,2,2,1536]{3,2,1,0:T(2,128)(2,1)S(1)}, bf16[1,2,2,1536]{3,2,1,0:T(2,128)(2,1)}, u32[]{:S(2)}) copy-start(bf16[1,2,2,1536]{3,2,1,0:T(2,128)(2,1)} %param.13) | copy-start | bytes 36868
  11.6 3.4 %copy-start.4 = (bf16[2,2,1536]{2,1,0:T(2,128)(2,1)S(1)}, bf16[2,2,1536]{2,1,0:T(2,128)(2,1)}, u32[]{:S(2)}) copy-start(bf16[2,2,1536]{2,1,0:T(2,128)(2,1)} %param.21) | copy-start | bytes 36868
  11.6 4.0 %copy-start.5 = (bf16[1,2,1536]{2,1,0:T(2,128)(2,1)S(1)}, bf16[1,2,1536]{2,1,0:T(2,128)(2,1)}, u32[]{:S(2)}) copy-start(bf16[1,2,1536]{2,1,0:T(2,128)(2,1)} %param.14) | copy-start | bytes 18436
  92.3 4.6 %copy-start.2 = (f32[64,128]{1,0:T(8,128)S(1)}, f32[64,128]{1,0:T(8,128)}, u32[]{:S(2)}) copy-start(f32[64,128]{1,0:T(8,128)} %get-tuple-element.8) | copy-start | bytes 98308

commit v2 on v1

--- a/solution.py
+++ b/solution.py
@@ -1,4 +1,5 @@
 import functools
+import math
 import jax
 import jax.numpy as jnp
 from jax import lax
@@ -7,6 +8,7 @@
 from jax.sharding import PartitionSpec as P
 
 HEAD_DIM = 64
+QUERY_SCALE = HEAD_DIM ** (-0.5) * math.log2(math.e)
 LANES = 128
 TEXT_PAD = 256
 norm_eps = 1e-06
@@ -22,11 +24,11 @@
 
 
 def kernel(
-    n_blk, n_head, piece, rows,
+    n_blk, n_head, piece, rows, padded,
     x_ref, mod_ref, gate_ref, wqkv_ref, wout_ref, stale_ref, text_ref, bias_ref,
     fmod_ref, fw_ref, latent_ref,
     recv_ref, fresh_out_ref, latent_out_ref,
-    kv, queries, fresh, attended, part_send, part_land, own_out, vel_own, vel_land, guided_ref,
+    kv, queries, fresh, attended, part_send, part_land, own_out, vel_own, vel_land, stat_own, stat_land, guided_ref, fw_pad,
     stale_send, stale_recv, own_sem, fresh_send, fresh_recv, fresh_own,
     part_ssem, part_rsem, sec_ssem, sec_rsem, vel_ssem, vel_rsem,
 ):
@@ -76,8 +78,9 @@
         centered = x - mean
         var = jnp.mean(centered * centered, axis=-1, keepdims=True)
         inv = 1.0 / jnp.sqrt(var + norm_eps)
-        normed = (centered * inv * (1.0 + mod_ref[s, 1:2, :]) + mod_ref[s, 0:1, :]).astype(BF16)
-        queries[s] = (dot(normed, wqkv_ref[0]).astype(BF16) * 0.125).astype(BF16)
+        shift_scale = mod_ref[s].astype(F32)
+        normed = (centered * inv * (1.0 + shift_scale[1:2]) + shift_scale[0:1]).astype(BF16)
+        queries[s] = (dot(normed, wqkv_ref[0]) * QUERY_SCALE).astype(BF16)
         for j in range(2):
             new = dot(normed, wqkv_ref[j + 1]).astype(BF16)
             kv[s, j, 0:TEXT_PAD, :] = text_ref[s, j]
@@ -105,18 +108,21 @@
     own_fresh.start()
 
     shift_term, scale_terms = [], []
-    for s in range(seqs):
-        lhs = jnp.broadcast_to(fmod_ref[s, 0:1, :], (8, width)).astype(BF16)
+    zeros = jnp.zeros(fw_ref.shape, BF16)
+    for s in range(seqs):
+        fw_pad[s] = jnp.concatenate([fw_ref[...], zeros] if s == 0 else [zeros, fw_ref[...]], axis=0)
+        final_wide = fmod_ref[s].astype(F32)
+        lhs = jnp.broadcast_to(final_wide[0:1], (8, width)).astype(BF16)
         shift_term.append(
-            lax.dot_general(lhs, fw_ref[s], NT, preferred_element_type=F32)[0:1]
+            lax.dot_general(lhs, fw_pad[s], NT, preferred_element_type=F32)[0:1]
         )
         terms = []
         for g in range(n_head):
             cut = slice(g * group, (g + 1) * group)
-            wide = jnp.broadcast_to(1.0 + fmod_ref[s, 1:2, cut], (8, group))
+            wide = jnp.broadcast_to(1.0 + final_wide[1:2, cut], (8, group))
             high = wide.astype(BF16)
             low = (wide - high.astype(F32)).astype(BF16)
-            w = fw_ref[s, :, cut]
+            w = fw_pad[s, :, cut]
             terms.append(
                 (
                     lax.dot_general(high, w, NT, preferred_element_type=F32)
@@ -129,109 +135,138 @@
     low_half = lane < HEAD_DIM
     share = pl.ds(pl.multiple_of(head * group, LANES), group)
     part_copies = []
+    ones = jnp.ones((base - TEXT_PAD + n_blk * piece, LANES), BF16)
     for s in range(seqs):
         own_copies[s].wait()
         for d in range(1, n_blk):
             stale_copies[s * (n_blk - 1) + d - 1].wait_recv()
-        bias = bias_ref[s]
-        for p in range(group // LANES):
-            cut = slice(p * LANES, (p + 1) * LANES)
-            q = queries[s, :, cut]
-            k = kv[s, 0, :, cut]
-            v = kv[s, 1, :, cut]
-            outs = []
-            for side in (low_half, jnp.logical_not(low_half)):
-                q_side = q * side.astype(BF16)
-                scores = lax.dot_general(q_side, k, NT, preferred_element_type=F32) + bias
-                top = jnp.max(scores, axis=-1, keepdims=True)
-                weights = jnp.exp(scores - top)
-                total = jnp.sum(weights, axis=-1, keepdims=True)
-                outs.append(dot(weights.astype(BF16), v) / total)
-            attended[s, :, cut] = jnp.where(low_half, outs[0], outs[1]).astype(BF16)
-        att = attended[s]
-        for g in range(n_head):
-            part_send[s, g] = dot(att, wout_ref[:, g * group : (g + 1) * group]).astype(BF16)
-        for d in range(1, n_head):
-            dst = lax.rem(head + d, n_head)
+        for c in range(2):
+            chunk = slice(c * half, (c + 1) * half)
+            for p in range(group // LANES):
+                cut = slice(p * LANES, (p + 1) * LANES)
+                q = queries[s, chunk, cut]
+                pair = jnp.concatenate(
+                    [q * low_half.astype(BF16), q * jnp.logical_not(low_half).astype(BF16)], axis=0
+                )
+                text_scores = (
+                    lax.dot_general(pair, kv[s, 0, 0:TEXT_PAD, cut], NT, preferred_element_type=F32)
+                    + bias_ref[s, :, 0:TEXT_PAD]
+                )
+                scores = lax.dot_general(
+                    pair, kv[s, 0, TEXT_PAD:, cut], NT, preferred_element_type=F32
+                )
+                if padded:
+                    scores = scores + bias_ref[s, :, TEXT_PAD:]
+                top = jnp.maximum(
+                    jnp.max(text_scores, axis=-1, keepdims=True),
+                    jnp.max(scores, axis=-1, keepdims=True),
+                )
+                text_weights = jnp.exp2(text_scores - top).astype(BF16)
+                weights = jnp.exp2(scores - top).astype(BF16)
+                text_v = jnp.concatenate([kv[s, 1, 0:TEXT_PAD, cut], ones[0:TEXT_PAD]], axis=1)
+                v = jnp.concatenate([kv[s, 1, TEXT_PAD:, cut], ones], axis=1)
+                acc = dot(text_weights, text_v) + dot(weights, v)
+                out = acc[:, 0:LANES] / acc[:, LANES : 2 * LANES]
+                attended[s, chunk, cut] = jnp.where(low_half, out[0:half], out[half:tokens]).astype(
+                    BF16
+                )
+            att = attended[s, chunk]
+            for g in range(n_head):
+                part_send[s, c, g] = dot(att, wout_ref[:, g * group : (g + 1) * group]).astype(BF16)
+            for d in range(1, n_head):
+                dst = lax.rem(head + d, n_head)
+                copy = pltpu.make_async_remote_copy(
+                    src_ref=part_send.at[s, c, dst],
+                    dst_ref=part_land.at[s, c, d - 1],
+                    send_sem=part_ssem.at[s, c, d - 1],
+                    recv_sem=part_rsem.at[s, c, d - 1],
+                    device_id={"head": dst},
+                )
+                copy.start()
+                part_copies.append(copy)
+
+    sec_copies = []
+    for s in range(seqs):
+        for c in range(2):
+            chunk = slice(c * half, (c + 1) * half)
+            total = part_send[s, c, head].astype(F32)
+            for d in range(1, n_head):
+                part_copies[(s * 2 + c) * (n_head - 1) + d - 1].wait_recv()
+                total = total + part_land[s, c, d - 1].astype(F32)
+            gate = gate_ref[:, share].astype(F32)[s : s + 1]
+            own_out[s, chunk] = (x_ref[s, chunk, share].astype(F32) + gate * total).astype(BF16)
             copy = pltpu.make_async_remote_copy(
-                src_ref=part_send.at[s, dst],
-                dst_ref=part_land.at[s, d - 1],
-                send_sem=part_ssem.at[s, d - 1],
-                recv_sem=part_rsem.at[s, d - 1],
-                device_id={"head": dst},
+                src_ref=own_out.at[s, chunk],
+                dst_ref=recv_ref.at[s, chunk],
+                send_sem=sec_ssem.at[s, c],
+                recv_sem=sec_rsem.at[s, c],
+                device_id={"section": 1 - sec},
             )
             copy.start()
-            part_copies.append(copy)
-
-    sec_copies = []
-    for s in range(seqs):
-        total = part_send[s, head].astype(F32)
-        for d in range(1, n_head):
-            part_copies[s * (n_head - 1) + d - 1].wait_recv()
-            total = total + part_land[s, d - 1].astype(F32)
-        own_out[s] = (x_ref[s, :, share].astype(F32) + gate_ref[s, :, share] * total).astype(BF16)
-        copy = pltpu.make_async_remote_copy(
-            src_ref=own_out.at[s],
-            dst_ref=recv_ref.at[s],
-            send_sem=sec_ssem.at[s],
-            recv_sem=sec_rsem.at[s],
-            device_id={"section": 1 - sec},
-        )
-        copy.start()
-        sec_copies.append(copy)
+            sec_copies.append(copy)
 
     wide_lane = lax.broadcasted_iota(jnp.int32, (half, LANES), 1)
     stats = jnp.zeros((half, LANES), F32)
     product = jnp.zeros((half, LANES), F32)
     first = sec == 0
     for s in range(seqs):
-        sec_copies[s].wait_recv()
+        for c in range(2):
+            sec_copies[s * 2 + c].wait_recv()
         x = jnp.where(
             first, recv_ref[s, 0:half].astype(F32), own_out[s, half:tokens].astype(F32)
         )
         mean = jnp.mean(x, axis=-1, keepdims=True)
         centered = x - mean
         squares = jnp.sum(centered * centered, axis=-1, keepdims=True)
-        scaled = (centered * (1.0 + fmod_ref[s, 1:2, share])).astype(BF16)
+        scaled = (centered * (1.0 + fmod_ref[s, :, share].astype(F32)[1:2])).astype(BF16)
         product = product + lax.dot_general(
-            scaled, fw_ref[s, :, share], NT, preferred_element_type=F32
+            scaled, fw_pad[s, :, share], NT, preferred_element_type=F32
         )
         stats = jnp.where(wide_lane == 2 * s, mean, stats)
         stats = jnp.where(wide_lane == 2 * s + 1, squares, stats)
-    vel_own[:, 0:LANES] = product
-    vel_own[:, LANES : 2 * LANES] = stats
+    vel_own[...] = product.astype(BF16)
+    stat_own[...] = stats.T[0:8]
     vel_copies = []
     for d in range(1, n_head):
-        copy = pltpu.make_async_remote_copy(
-            src_ref=vel_own,
-            dst_ref=vel_land.at[head],
-            send_sem=vel_ssem.at[d - 1],
-            recv_sem=vel_rsem.at[d - 1],
-            device_id={"head": lax.rem(head + d, n_head)},
-        )
-        copy.start()
-        vel_copies.append(copy)
+        for j, (src, land) in enumerate(((vel_own, vel_land), (stat_own, stat_land))):
+            copy = pltpu.make_async_remote_copy(
+                src_ref=src,
+                dst_ref=land.at[head],
+                send_sem=vel_ssem.at[j, d - 1],
+                recv_sem=vel_rsem.at[j, d - 1],
+                device_id={"head": lax.rem(head + d, n_head)},
+            )
+            copy.start()
+            vel_copies.append(copy)
+    vel_land[head] = vel_own[...]
+    stat_land[head] = stat_own[...]
     for copy in vel_copies:
         copy.wait_recv()
-    vel_land[head] = vel_own[...]
-    velocity = jnp.zeros((half, LANES), F32)
-    summed = vel_land[0, :, 0:LANES]
+    summed = vel_land[0].astype(F32)
     for g in range(1, n_head):
-        summed = summed + vel_land[g, :, 0:LANES]
-    for s in range(seqs):
-        means = [vel_land[g, :, LANES + 2 * s : LANES + 2 * s + 1] for g in range(n_head)]
+        summed = summed + vel_land[g].astype(F32)
+    row = lax.broadcasted_iota(jnp.int32, (LANES, half), 0)
+    packed = jnp.zeros((LANES, half), F32)
+    for s in range(seqs):
+        means = [stat_land[g, 2 * s : 2 * s + 1, :] for g in range(n_head)]
         mean = sum(means) / n_head
         var = sum(
-            vel_land[g, :, LANES + 2 * s + 1 : LANES + 2 * s + 2]
-            + group * (means[g] - mean) * (means[g] - mean)
+            stat_land[g, 2 * s + 1 : 2 * s + 2, :] + group * (means[g] - mean) * (means[g] - mean)
             for g in range(n_head)
         ) / width
-        inv = 1.0 / jnp.sqrt(var + norm_eps)
+        first_row = s * (n_head + 1)
+        packed = jnp.where(row == first_row, 1.0 / jnp.sqrt(var + norm_eps), packed)
+        for g in range(n_head):
+            packed = jnp.where(row == first_row + 1 + g, means[g] - mean, packed)
+    columns = packed.T
+    velocity = jnp.zeros((half, LANES), F32)
+    for s in range(seqs):
+        at = s * (n_head + 1)
         mine = low_half if s == 0 else jnp.logical_not(low_half)
         corrected = jnp.where(mine, summed, 0.0)
         for g in range(n_head):
-            corrected = corrected + (means[g] - mean) * scale_terms[s][g]
-        velocity = velocity + corrected * inv + shift_term[s]
+            corrected = corrected + columns[:, at + 1 + g : at + 2 + g] * scale_terms[s][g]
+        velocity = velocity + corrected * columns[:, at : at + 1] + shift_term[s]
     weighted = velocity * jnp.where(low_half, guidance, 1.0 - guidance)
     guided_ref[...] = weighted + pltpu.roll(weighted, HEAD_DIM, 1)
     even = guided_ref[pl.ds(0, half // 2, 2), :]
@@ -283,17 +318,12 @@
         (position - base) % piece < kept,
     )
     bias = jnp.where(counted, 0.0, -1e30).astype(F32)[:, None, :]
-    weight_t = final_weight.T
-    out_ch = weight_t.shape[0]
-    final_t = jnp.stack(
-        [jnp.pad(weight_t, ((0, out_ch), (0, 0))), jnp.pad(weight_t, ((out_ch, 0), (0, 0)))]
-    )
     fresh_type = BF16 if rows % 16 == 0 else F32
     half = tokens // 2
     vmem = pl.BlockSpec(memory_space=pltpu.VMEM)
     dma = pltpu.SemaphoreType.DMA
     received, fresh, latent_next = pl.pallas_call(
-        functools.partial(kernel, n_blk, n_head, piece, rows),
+        functools.partial(kernel, n_blk, n_head, piece, rows, piece != kept),
         out_shape=(
             jax.ShapeDtypeStruct((seqs, tokens, group), BF16),
             jax.ShapeDtypeStruct((all_seqs, 2, rows, group), fresh_type),
@@ -306,39 +336,42 @@
             pltpu.VMEM((seqs, tokens, group), BF16),
             pltpu.VMEM((seqs, 2, tokens, group), fresh_type),
             pltpu.VMEM((seqs, tokens, group), BF16),
-            pltpu.VMEM((seqs, n_head, tokens, group), BF16),
-            pltpu.VMEM((seqs, n_head - 1, tokens, group), BF16),
+            pltpu.VMEM((seqs, 2, n_head, half, group), BF16),
+            pltpu.VMEM((seqs, 2, n_head - 1, half, group), BF16),
             pltpu.VMEM((seqs, tokens, group), BF16),
-            pltpu.VMEM((half, 2 * LANES), F32),
-            pltpu.VMEM((n_head, half, 2 * LANES), F32),
+            pltpu.VMEM((half, LANES), BF16),
+            pltpu.VMEM((n_head, half, LANES), BF16),
+            pltpu.VMEM((8, half), F32),
+            pltpu.VMEM((n_head, 8, half), F32),
             pltpu.VMEM((half, LANES), F32),
+            pltpu.VMEM((seqs, LANES, width), BF16),
             dma((seqs, n_blk - 1)),
             dma((seqs, n_blk - 1)),
             dma((seqs,)),
             dma((n_blk - 1,)),
             dma((n_blk - 1,)),
             dma(()),
-            dma((seqs, n_head - 1)),
-            dma((seqs, n_head - 1)),
-            dma((seqs,)),
-            dma((seqs,)),
-            dma((n_head - 1,)),
-            dma((n_head - 1,)),
+            dma((seqs, 2, n_head - 1)),
+            dma((seqs, 2, n_head - 1)),
+            dma((seqs, 2)),
+            dma((seqs, 2)),
+            dma((2, n_head - 1)),
+            dma((2, n_head - 1)),
         ],
         compiler_params=pltpu.CompilerParams(
             collective_id=0, has_side_effects=True, vmem_limit_bytes=56 * 1024 * 1024
         ),
     )(
         x,
-        modulation[0].astype(F32),
-        attn_gate[0].astype(F32)[:, None, :],
+        modulation[0],
+        attn_gate[0],
         qkv_weight[0].transpose(1, 0, 2),
         out_weight[0],
         stale,
         text,
         bias,
-        final_mod.astype(F32),
-        final_t,
+        final_mod,
+        final_weight.T,
         latent[0],
     )
     cache_patch = fresh.astype(BF16).transpose(0, 2, 1, 3)

time: 97.8 us -> 85.1 us (0.87)
  the two profiles are of different devices: /device:TPU:29 before, /device:TPU:1 now
where the time goes in v2:
time: 85.1 us; the launch traced here: 84.9 us
  Pallas kernels  66.4 us (78%)
  other arithmetic  9.16 us (11%)
  local copies, waits for them, and re-layouts  8.67 us (10%)
    pallas_call x1, Pallas kernels, shards(): pl.pallas_call(functools.partial(kernel, n_blk, n_head, piece, rows, piec...  66.4 us
    unnamed x10, local copies, waits for them, and re-layouts  5.3 us
    transpose x1, other arithmetic, shards(): stale = stale.transpose(0, 3, 1, 2, 4).reshape(all_seqs, 2, kept, group)  4.02 us
    select_n x1, other arithmetic, shards(): jnp.where(j < at[:, :, 0], cache[:, :, j], cache[:, :, j + 1])  3.54 us
    transpose x1, local copies, waits for them, and re-layouts, shards(): stale = stale.transpose(0, 3, 1, 2, 4).reshape(all_seqs, 2, kept, group)  1.93 us

profile of v2, /device:TPU:1, one launch (start us, length us, event | category | flops | bytes accessed | tf_op | source)
XLA Modules:
  0.0 84.9 jit_solution(12116931381630077963)
XLA Ops:
  0.6 0.9 %compare_reduce_fusion.2 = (pred[4]{0:T(512)(128)(4,1)S(1)}, pred[4]{0:T(512)(128)(4,1)S(1)}, pred[4]{0:T(512)(128)(4,1)S(1)}) fusion(s32[4,4]{1,0:T(4,128)} %param.20, s32[]{:T(128)S(6)} %select_n.69), kind=kLoop, calls=%fused_computation.20 | loop fusion | flops 12 | bytes 32 | tf_op jit(solution)/shard_map/gt | solution.py:301
  1.5 0.1 broadcast_in_dim.61
  1.6 0.1 gt.47
  1.7 0.1 broadcast_in_dim.63
  1.8 0.1 gt.50
  1.9 0.1 broadcast_in_dim.65
  1.9 0.1 gt.53
  2.0 3.5 %broadcast_select_fusion.2 = (bf16[8,1,64,2,384]{4,3,2,0,1:T(2,128)(2,1)S(1)}, bf16[8,1,64,2,384]{4,3,2,0,1:T(2,128)(2,1)S(1)}, bf16[8,1,64,2,384]{4,3,2,0,1:T(2,128)(2,1)S(1)}) fusion(pred[8]{0:T(512)(128)(4,1)S(1)} %gt.47, bf16[8,64,4,2,384]{4,3,2,1,0:T(2,128)(2,1)} %bitcast.51, pred[8]{0:T(512)(128)(4,1)S(1)} %gt.53, pred[8]{0:T(512)(128)(4,1)S(1)} %gt.50), kind=kLoop, calls=%fused_computation.3 | loop fusion | flops 1179648 | bytes 5505048 | tf_op jit(solution)/shard_map/jit(_where)/select_n | solution.py:301
  5.6 4.0 %maximum_bitcast_fusion = bf16[8,2,3,64,384]{4,1,3,0,2:T(2,128)(2,1)S(1)} fusion(bf16[8,1,64,2,384]{4,3,2,0,1:T(2,128)(2,1)S(1)} %get-tuple-element.16, bf16[8,1,64,2,384]{4,3,2,0,1:T(2,128)(2,1)S(1)} %get-tuple-element.17, bf16[8,1,64,2,384]{4,3,2,0,1:T(2,128)(2,1)S(1)} %get-tuple-element.15), kind=kLoop, calls=%fused_computation | loop fusion | flops 2359296 | bytes 4718592 | tf_op jit(solution)/shard_map/transpose | solution.py:306
  9.6 0.0 copy-start.2
  9.6 0.0 copy-start
  9.6 1.9 %copy.18 = bf16[8,2,3,64,384]{4,3,2,1,0:T(8,128)(2,1)} copy(bf16[8,2,3,64,384]{4,1,3,0,2:T(2,128)(2,1)S(1)} %maximum_bitcast_fusion) | data formatting | bytes 4718592 | tf_op jit(solution)/shard_map/transpose | solution.py:306
  11.6 0.0 copy-done.2
  11.6 0.7 select_select_fusion.bias_ref
  12.3 0.0 copy-done
  12.3 0.1 copy.25
  12.3 1.0 %pad.4.text_ref = bf16[2,2,256,384]{3,2,1,0:T(8,128)(2,1)} pad(bf16[2,2,154,384]{3,2,1,0:T(8,128)(2,1)S(1)} %bitcast.52, bf16[]{:T(256)} %constant.35.clone.1), padding=0_0x0_0x0_102x0_0 | pad | bytes 1259522 | tf_op jit(solution)/shard_map/jit(_pad)/pad | solution.py:309
  13.3 66.4 %shard_map.139 = (bf16[2,256,384]{2,1,0:T(8,128)(2,1)}, bf16[8,2,64,384]{3,2,1,0:T(8,128)(2,1)}, f32[64,128]{1,0:T(8,128)}) custom-call(bf16[2,256,1536]{2,1,0:T(8,128)(2,1)} %bitcast.53, bf16[2,2,1536]{2,1,0:T(2,128)(2,1)} %bitcast.60, bf16[2,1536]{1,0:T(2,128)(2,1)} %bitcast.61, bf16[3,1536,384]{2,1,0:T(8,128)(2,1)} %bitcast.50, ...), custom_call_target="tpu_custom_call" | custom-call | tf_op jit(solution)/shard_map/pallas_call | solution.py:325
  79.7 0.0 copy-start.1
  79.7 2.8 %copy.20 = bf16[1,8,64,2,384]{4,3,2,1,0:T(2,128)(2,1)} copy(bf16[1,8,64,2,384]{4,2,3,1,0:T(8,128)(2,1)} %bitcast.55) | data formatting | bytes 1572864
  82.5 1.8 %copy.28 = bf16[1,2,256,384]{3,2,1,0:T(8,128)(2,1)} copy(bf16[1,2,256,384]{3,2,1,0:T(8,128)(2,1)} %bitcast.56) | data formatting | bytes 786432
  84.3 0.0 copy-done.1
  84.3 0.6 copy.29
  (2 shorter events, 0.0 us)
Async XLA Ops:
  9.6 2.0 %copy-start.2 = (s32[2]{0:T(128)S(1)}, s32[2]{0:T(128)}, u32[]{:S(2)}) copy-start(s32[2]{0:T(128)} %param.19) | copy-start | bytes 28
  9.6 2.7 %copy-start = (bf16[1,2,154,2,384]{4,3,2,1,0:T(2,128)(2,1)S(1)}, bf16[1,2,154,2,384]{4,3,2,1,0:T(2,128)(2,1)}, u32[]{:S(2)}) copy-start(bf16[1,2,154,2,384]{4,3,2,1,0:T(2,128)(2,1)} %param.18) | copy-start | bytes 1419268
  79.7 4.6 %copy-start.1 = (f32[64,128]{1,0:T(8,128)S(1)}, f32[64,128]{1,0:T(8,128)}, u32[]{:S(2)}) copy-start(f32[64,128]{1,0:T(8,128)} %get-tuple-element.8) | copy-start | bytes 98308

commit v3 on v2

--- a/solution.py
+++ b/solution.py
@@ -62,7 +62,8 @@
                 recv_sem=stale_recv.at[s, d - 1],
                 device_id={"blk": dst},
             )
-            copy.start()
+            if s == 0:
+                copy.start()
             stale_copies.append(copy)
     own_copies = []
     for s in range(seqs):
@@ -87,25 +88,10 @@
             kv[s, j, TEXT_PAD:base, :] = new
             fresh[s, j] = new.astype(fresh.dtype)
 
-    def fresh_rows(dst):
-        return pl.ds(pl.multiple_of(dst * rows, 8), rows)
-
-    fresh_copies = []
-    for d in range(1, n_blk):
-        dst = lax.rem(blk + d, n_blk)
-        copy = pltpu.make_async_remote_copy(
-            src_ref=fresh.at[:, :, fresh_rows(dst), :],
-            dst_ref=fresh_out_ref.at[pl.ds(blk * seqs, seqs)],
-            send_sem=fresh_send.at[d - 1],
-            recv_sem=fresh_recv.at[d - 1],
-            device_id={"blk": dst},
-        )
+    for copy in stale_copies[: n_blk - 1]:
+        copy.wait_send()
+    for copy in stale_copies[n_blk - 1 :]:
         copy.start()
-        fresh_copies.append(copy)
-    own_fresh = pltpu.make_async_copy(
-        fresh.at[:, :, fresh_rows(blk), :], fresh_out_ref.at[pl.ds(blk * seqs, seqs)], fresh_own
-    )
-    own_fresh.start()
 
     shift_term, scale_terms = [], []
     zeros = jnp.zeros(fw_ref.shape, BF16)
@@ -134,6 +120,10 @@
     lane = lax.broadcasted_iota(jnp.int32, (1, LANES), 1)
     low_half = lane < HEAD_DIM
     share = pl.ds(pl.multiple_of(head * group, LANES), group)
+    def fresh_rows(dst):
+        return pl.ds(pl.multiple_of(dst * rows, 8), rows)
+
+    fresh_copies = []
     part_copies = []
     ones = jnp.ones((base - TEXT_PAD + n_blk * piece, LANES), BF16)
     for s in range(seqs):
@@ -184,6 +174,22 @@
                 )
                 copy.start()
                 part_copies.append(copy)
+        if s == 0:
+            for d in range(1, n_blk):
+                dst = lax.rem(blk + d, n_blk)
+                copy = pltpu.make_async_remote_copy(
+                    src_ref=fresh.at[:, :, fresh_rows(dst), :],
+                    dst_ref=fresh_out_ref.at[pl.ds(blk * seqs, seqs)],
+                    send_sem=fresh_send.at[d - 1],
+                    recv_sem=fresh_recv.at[d - 1],
+                    device_id={"blk": dst},
+                )
+                copy.start()
+                fresh_copies.append(copy)
+            own_fresh = pltpu.make_async_copy(
+                fresh.at[:, :, fresh_rows(blk), :], fresh_out_ref.at[pl.ds(blk * seqs, seqs)], fresh_own
+            )
+            own_fresh.start()
 
     sec_copies = []
     for s in range(seqs):
@@ -276,7 +282,7 @@
     own_fresh.wait()
     for copy in fresh_copies:
         copy.wait()
-    for copy in stale_copies + part_copies + sec_copies + vel_copies:
+    for copy in stale_copies[n_blk - 1 :] + part_copies + sec_copies + vel_copies:
         copy.wait_send()
 
 
@@ -295,14 +301,8 @@
     all_seqs, rows, patches = cache.shape[:3]
     kept = (patches - 1) * rows
     piece = -(-kept // 16) * 16
-    at = seq_patch[:, None, None, None, None]
-    stale = jnp.stack(
-        [
-            jnp.where(j < at[:, :, 0], cache[:, :, j], cache[:, :, j + 1])
-            for j in range(patches - 1)
-        ],
-        axis=1,
-    )
+    before = jnp.arange(patches - 1, dtype=jnp.int32)[None, :] < seq_patch[:, None]
+    stale = jnp.where(before[:, None, :, None, None], cache[:, :, :-1], cache[:, :, 1:])
     stale = stale.transpose(0, 3, 1, 2, 4).reshape(all_seqs, 2, kept, group)
     stale = jnp.pad(stale, ((0, 0), (0, 0), (0, piece - kept), (0, 0)))
     text_count = text_kv.shape[2]

time: 85.1 us -> 81.2 us (0.954)
  other arithmetic: 9.16 us -> 1.13 us
  local copies, waits for them, and re-layouts: 8.67 us -> 12.8 us
    unnamed x10 -> x13, local copies, waits for them, and re-layouts: 5.3 us -> 9.72 us
    transpose x1 -> x0, other arithmetic: 4.02 us -> none  [shards(): stale = stale.transpose(0, 3, 1, 2, 4).reshape(all_seqs, 2, kept, group)]
    select_n x1, other arithmetic: 3.54 us -> 0.41 us  [shards(): jnp.where(before[:, None, :, None, None], cache[:, :, :-1], cache[:, :, 1:])]
    transpose x1 -> x0, local copies, waits for them, and re-layouts: 1.93 us -> none  [shards(): stale = stale.transpose(0, 3, 1, 2, 4).reshape(all_seqs, 2, kept, group)]
    reshape x0 -> x1, local copies, waits for them, and re-layouts: none -> 1.81 us  [shards(): stale = stale.transpose(0, 3, 1, 2, 4).reshape(all_seqs, 2, kept, group)]
    gt x1 -> x0, other arithmetic: 0.9 us -> none  [shards(): j < at[:, :, 0]]
where the time goes in v3:
time: 81.2 us; the launch traced here: 81 us
  Pallas kernels  66.3 us (82%)
  local copies, waits for them, and re-layouts  12.8 us (16%)
  other arithmetic  1.13 us (1%)
    pallas_call x1, Pallas kernels, shards(): pl.pallas_call(functools.partial(kernel, n_blk, n_head, piece, rows, piec...  66.3 us
    unnamed x13, local copies, waits for them, and re-layouts  9.72 us
    reshape x1, local copies, waits for them, and re-layouts, shards(): stale = stale.transpose(0, 3, 1, 2, 4).reshape(all_seqs, 2, kept, group)  1.81 us

profile of v3, /device:TPU:1, one launch (start us, length us, event | category | flops | bytes accessed | tf_op | source)
XLA Modules:
  0.0 81.0 jit_solution(18200675484578915747)
XLA Ops:
  0.6 0.0 copy-start
  0.6 0.7 copy-done
  1.3 0.2 dynamic-slice_reduce_fusion
  1.5 0.1 broadcast_in_dim.49
  1.6 0.1 lt.68
  1.7 3.7 %copy.24 = bf16[1,8,64,4,2,384]{5,1,3,2,4,0:T(8,128)(2,1)S(1)} copy(bf16[1,8,64,4,2,384]{5,4,3,2,1,0:T(2,128)(2,1)} %param.17) | data formatting | bytes 6291456 | tf_op args[5]
  5.4 0.4 slice_select_fusion
  5.8 0.0 copy-start.3
  5.8 0.0 copy-start.1
  5.9 1.8 %copy.20.stale_ref = bf16[8,2,192,384]{3,2,1,0:T(8,128)(2,1)} copy(bf16[8,2,192,384]{3,0,2,1:T(8,128)(2,1)S(1)} %bitcast.26) | data formatting | bytes 4718592 | tf_op jit(solution)/shard_map/reshape | solution.py:306
  7.7 0.0 copy-done.3
  7.7 0.7 select_select_fusion.bias_ref
  8.4 0.0 copy-done.1
  8.4 0.1 copy.25
  8.5 1.0 %pad.4.text_ref = bf16[2,2,256,384]{3,2,1,0:T(8,128)(2,1)} pad(bf16[2,2,154,384]{3,2,1,0:T(8,128)(2,1)S(1)} %bitcast.28, bf16[]{:T(256)} %constant.30.clone.1), padding=0_0x0_0x0_102x0_0 | pad | bytes 1259522 | tf_op jit(solution)/shard_map/jit(_pad)/pad | solution.py:309
  9.4 66.3 %shard_map.139 = (bf16[2,256,384]{2,1,0:T(8,128)(2,1)}, bf16[8,2,64,384]{3,2,1,0:T(8,128)(2,1)}, f32[64,128]{1,0:T(8,128)}) custom-call(bf16[2,256,1536]{2,1,0:T(8,128)(2,1)} %bitcast.29, bf16[2,2,1536]{2,1,0:T(2,128)(2,1)} %bitcast.36, bf16[2,1536]{1,0:T(2,128)(2,1)} %bitcast.37, bf16[3,1536,384]{2,1,0:T(8,128)(2,1)} %bitcast.27, ...), custom_call_target="tpu_custom_call" | custom-call | tf_op jit(solution)/shard_map/pallas_call | solution.py:325
  75.7 0.0 copy-start.2
  75.8 2.8 %copy.21 = bf16[1,8,64,2,384]{4,3,2,1,0:T(2,128)(2,1)} copy(bf16[1,8,64,2,384]{4,2,3,1,0:T(8,128)(2,1)} %bitcast.31) | data formatting | bytes 1572864
  78.6 1.8 %copy.28 = bf16[1,2,256,384]{3,2,1,0:T(8,128)(2,1)} copy(bf16[1,2,256,384]{3,2,1,0:T(8,128)(2,1)} %bitcast.32) | data formatting | bytes 786432
  80.4 0.0 copy-done.2
  80.4 0.6 copy.29
  (3 shorter events, 0.0 us)
Async XLA Ops:
  0.6 0.7 copy-start
  5.8 1.9 %copy-start.3 = (s32[2]{0:T(128)S(1)}, s32[2]{0:T(128)}, u32[]{:S(2)}) copy-start(s32[2]{0:T(128)} %param.19) | copy-start | bytes 28
  5.8 2.6 %copy-start.1 = (bf16[1,2,154,2,384]{4,3,2,1,0:T(2,128)(2,1)S(1)}, bf16[1,2,154,2,384]{4,3,2,1,0:T(2,128)(2,1)}, u32[]{:S(2)}) copy-start(bf16[1,2,154,2,384]{4,3,2,1,0:T(2,128)(2,1)} %param.18) | copy-start | bytes 1419268
  75.7 4.6 %copy-start.2 = (f32[64,128]{1,0:T(8,128)S(1)}, f32[64,128]{1,0:T(8,128)}, u32[]{:S(2)}) copy-start(f32[64,128]{1,0:T(8,128)} %get-tuple-element.8) | copy-start | bytes 98308
